TPU v7x, 128 devices: a whole 4x4x4 slice. The times are simulated.
128 devices in a mesh: dp: 32 (over y, z_lo, x), mp: 4 (over z_hi, core).
Axes of the slice: x: 4, y: 4, z: 4 (z_hi: 2, z_lo: 2; z = z_hi * 2 + z_lo), core: 2. Of those that a mesh axis runs over, the one named last changes fastest.
Arguments:
- tags: bfloat16 [512, 128, 512], P('mp', 'dp'), may hold values from -6 to 6
- memory: bfloat16 [784, 128, 512], P('mp', 'dp'), may hold values from -6 to 6
- cotangent: bfloat16 [512, 128, 512], P('mp', 'dp'), may hold values from -6 to 6
- tag_lengths: int32 [128], P('dp'), may hold values from 64 to 512, as said below
- mem_lengths: int32 [128], P('dp'), may hold values from 392 to 784, as said below
- self_qkv: bfloat16 [512, 3, 512], P(None, None, 'mp'), may hold values from -0.25 to 0.25
- self_qv_bias: bfloat16 [2, 512], P(None, 'mp'), may hold values from -3 to 3
- self_out: bfloat16 [512, 512], P('mp'), may hold values from -2 to 2
- cross_q: bfloat16 [512, 512], P(None, 'mp'), may hold values from -0.25 to 0.25
- cross_kv: bfloat16 [512, 2, 512], P(None, None, 'mp'), may hold values from -0.25 to 0.25
- cross_qv_bias: bfloat16 [2, 512], P(None, 'mp'), may hold values from -3 to 3
- cross_out: bfloat16 [512, 512], P('mp'), may hold values from -2 to 2
- ffn_in: bfloat16 [512, 1024], P(None, 'mp'), may hold values from -0.25 to 0.25
- ffn_in_bias: bfloat16 [1024], P('mp'), may hold values from -3 to 3
- ffn_out: bfloat16 [1024, 512], P('mp'), may hold values from -0.25 to 0.25
- out_bias: bfloat16 [3, 512], replicated, may hold values from -3 to 3
- norm_gain: bfloat16 [3, 512], replicated, may hold values from 0.25 to 1.75
- norm_bias: bfloat16 [3, 512], replicated, may hold values from -3 to 3
Outputs:
- result: bfloat16 [512, 128, 512], P('mp', 'dp')
- tags_grad: bfloat16 [512, 128, 512], P('mp', 'dp')
- memory_grad: bfloat16 [784, 128, 512], P('mp', 'dp')
- grad_self_qkv: float32 [512, 3, 512], P(None, None, 'mp')
- grad_self_qv_bias: float32 [2, 512], P(None, 'mp')
- grad_self_out: float32 [512, 512], P('mp')
- grad_cross_q: float32 [512, 512], P(None, 'mp')
- grad_cross_kv: float32 [512, 2, 512], P(None, None, 'mp')
- grad_cross_qv_bias: float32 [2, 512], P(None, 'mp')
- grad_cross_out: float32 [512, 512], P('mp')
- grad_ffn_in: float32 [512, 1024], P(None, 'mp')
- grad_ffn_in_bias: float32 [1024], P('mp')
- grad_ffn_out: float32 [1024, 512], P('mp')
- grad_out_bias: float32 [3, 512], P(None, 'mp')
- grad_norm_gain: float32 [3, 512], P(None, 'mp')
- grad_norm_bias: float32 [3, 512], P(None, 'mp')
Inputs may be any that keep to these rules, and one draw needn't show every extreme that they name: `tag_lengths`: per table the number of real tags; in each aligned block of 4 tables (the tables of one index of dp) one table has exactly 512. `mem_lengths`: per table the number of valid memory tokens; in each aligned block of 4 tables one table has exactly 784.
All inputs are finite; a program needn't handle non-finite values.
Results may differ from a plain program's by a relative error of at most 0.04.
Values may be sent and summed in bfloat16 or wider, within the bound.
A program may use at most 128 MiB of HBM per device.

v0:
```python
import math

import jax
import jax.numpy as jnp
from jax import lax
from jax.sharding import PartitionSpec as P

HEAD = 128


EPSILON = 1e-05


def normalize(values, gain_row, shift_row):
    center = values - jnp.mean(values, axis=-1, keepdims=True)
    inverse = lax.rsqrt(jnp.mean(center * center, axis=-1, keepdims=True) + EPSILON)
    unit_values = center * inverse
    return (unit_values * gain_row + shift_row, unit_values, inverse)


def normalize_back(grad_in, unit_values, inverse, gain_row):
    scaled = grad_in * gain_row
    inner_term = (
        scaled
        - jnp.mean(scaled, axis=-1, keepdims=True)
        - unit_values * jnp.mean(scaled * unit_values, axis=-1, keepdims=True)
    )
    return (
        inverse * inner_term,
        jnp.sum(grad_in * unit_values, axis=(0, 1)),
        jnp.sum(grad_in, axis=(0, 1)),
    )


def attend_forward(queries, key_rows, values, allowed, scale_factor):
    scores = (
        jnp.einsum("qbhe,kbhe->bhqk", queries, key_rows, preferred_element_type=jnp.float32)
        * scale_factor
    )
    scores = jnp.where(allowed, scores, -1e30)
    row_peak = jnp.max(scores, axis=-1, keepdims=True)
    exp_scores = jnp.exp(scores - row_peak)
    row_total = jnp.sum(exp_scores, axis=-1, keepdims=True)
    attn_probs = (exp_scores / row_total).astype(jnp.bfloat16)
    output = jnp.einsum("bhqk,kbhe->qbhe", attn_probs, values, preferred_element_type=jnp.float32)
    return (output, row_peak + jnp.log(row_total))


def attend_back(queries, key_rows, values, allowed, log_total, out_grad, scale_factor):
    scores = (
        jnp.einsum("qbhe,kbhe->bhqk", queries, key_rows, preferred_element_type=jnp.float32)
        * scale_factor
    )
    scores = jnp.where(allowed, scores, -1e30)
    attn_probs = jnp.exp(scores - log_total)
    prob_grad = jnp.einsum("qbhe,kbhe->bhqk", out_grad, values, preferred_element_type=jnp.float32)
    score_grad = (
        attn_probs * (prob_grad - jnp.sum(attn_probs * prob_grad, axis=-1, keepdims=True))
    ).astype(jnp.bfloat16)
    query_grad = (
        jnp.einsum("bhqk,kbhe->qbhe", score_grad, key_rows, preferred_element_type=jnp.float32)
        * scale_factor
    )
    key_grad = (
        jnp.einsum("bhqk,qbhe->kbhe", score_grad, queries, preferred_element_type=jnp.float32)
        * scale_factor
    )
    value_grad = jnp.einsum(
        "bhqk,qbhe->kbhe",
        attn_probs.astype(jnp.bfloat16),
        out_grad,
        preferred_element_type=jnp.float32,
    )
    return (query_grad, key_grad, value_grad)


def per_device(
    tags,
    memory,
    cotangent,
    tag_lengths,
    mem_lengths,
    self_qkv,
    self_qv_bias,
    self_out,
    cross_q,
    cross_kv,
    cross_qv_bias,
    cross_out,
    ffn_in,
    ffn_in_bias,
    ffn_out,
    out_bias,
    norm_gain,
    norm_bias,
):
    local_len, tables, model_width = tags.shape
    local_width = self_qkv.shape[2]
    local_heads = local_width // HEAD
    scale_factor = 1.0 / math.sqrt(HEAD)

    def split_heads(values):
        return values.reshape(values.shape[0], tables, local_heads, HEAD)

    def join_heads(values):
        return values.reshape(values.shape[0], tables, local_width)

    gathered_tags, gathered_memory = (
        lax.all_gather(tags, "mp", axis=0, tiled=True),
        lax.all_gather(memory, "mp", axis=0, tiled=True),
    )
    seq_len = gathered_tags.shape[0]
    mem_len = gathered_memory.shape[0]
    positions = jnp.arange(seq_len)
    causal = positions[None, :] <= positions[:, None]
    live_keys = positions[None, :] < tag_lengths[:, None]
    self_allowed = causal[None, None, :, :] & live_keys[:, None, None, :]
    cross_allowed = (jnp.arange(mem_len)[None, :] < mem_lengths[:, None])[:, None, None, :]
    projected = jnp.einsum(
        "lbd,dch->lbch", gathered_tags, self_qkv, preferred_element_type=jnp.float32
    )
    self_query = (projected[:, :, 0] + self_qv_bias[0]).astype(jnp.bfloat16)
    self_key = projected[:, :, 1].astype(jnp.bfloat16)
    self_value = (projected[:, :, 2] + self_qv_bias[1]).astype(jnp.bfloat16)
    self_heads, self_lse = attend_forward(
        split_heads(self_query),
        split_heads(self_key),
        split_heads(self_value),
        self_allowed,
        scale_factor,
    )
    self_mixed = join_heads(self_heads).astype(jnp.bfloat16)
    self_term = jnp.einsum("lbh,hd->lbd", self_mixed, self_out, preferred_element_type=jnp.float32)
    attended = lax.psum_scatter(
        self_term.astype(jnp.bfloat16), "mp", scatter_dimension=0, tiled=True
    ).astype(jnp.float32)
    first_norm, first_unit, first_inv = normalize(
        tags.astype(jnp.float32) + attended + out_bias[0], norm_gain[0], norm_bias[0]
    )
    gathered_first = lax.all_gather(first_norm.astype(jnp.bfloat16), "mp", axis=0, tiled=True)
    cross_query = (
        jnp.einsum("lbd,dh->lbh", gathered_first, cross_q, preferred_element_type=jnp.float32)
        + cross_qv_bias[0]
    ).astype(jnp.bfloat16)
    mem_proj = jnp.einsum(
        "mbd,dch->mbch", gathered_memory, cross_kv, preferred_element_type=jnp.float32
    )
    cross_key = mem_proj[:, :, 0].astype(jnp.bfloat16)
    cross_value = (mem_proj[:, :, 1] + cross_qv_bias[1]).astype(jnp.bfloat16)
    cross_heads, cross_lse = attend_forward(
        split_heads(cross_query),
        split_heads(cross_key),
        split_heads(cross_value),
        cross_allowed,
        scale_factor,
    )
    cross_mixed = join_heads(cross_heads).astype(jnp.bfloat16)
    cross_term = jnp.einsum(
        "lbh,hd->lbd", cross_mixed, cross_out, preferred_element_type=jnp.float32
    )
    crossed = lax.psum_scatter(
        cross_term.astype(jnp.bfloat16), "mp", scatter_dimension=0, tiled=True
    ).astype(jnp.float32)
    second_norm, second_unit, second_inv = normalize(
        first_norm + crossed + out_bias[1], norm_gain[1], norm_bias[1]
    )
    second_low = second_norm.astype(jnp.bfloat16)
    ffn_rows = lax.all_gather(second_low, "mp", axis=0, tiled=True).reshape(-1, model_width)
    w_first, b_first, w_second = (ffn_in, ffn_in_bias, ffn_out)
    pre_act = jnp.dot(ffn_rows, w_first, preferred_element_type=jnp.float32) + b_first
    gelu_values, gelu_pull = jax.vjp(jax.nn.gelu, pre_act)
    hidden = gelu_values.astype(jnp.bfloat16)
    ffn_rows_out = jnp.dot(hidden, w_second, preferred_element_type=jnp.float32)
    ffn_term = lax.psum_scatter(
        ffn_rows_out.reshape(seq_len, tables, model_width).astype(jnp.bfloat16),
        "mp",
        scatter_dimension=0,
        tiled=True,
    ).astype(jnp.float32)
    result, third_unit, third_inv = normalize(
        second_norm + ffn_term + out_bias[2], norm_gain[2], norm_bias[2]
    )
    grad_third, gain_three, shift_three = normalize_back(
        cotangent.astype(jnp.float32), third_unit, third_inv, norm_gain[2]
    )
    bias_three = jnp.sum(grad_third, axis=(0, 1))
    grad_ffn = grad_third.astype(jnp.bfloat16)
    grad_rows = lax.all_gather(grad_ffn, "mp", axis=0, tiled=True).reshape(-1, model_width)
    grad_w_second = jnp.einsum("rf,rd->fd", hidden, grad_rows, preferred_element_type=jnp.float32)
    grad_hidden = jnp.einsum("rd,fd->rf", grad_rows, w_second, preferred_element_type=jnp.float32)
    grad_pre = gelu_pull(grad_hidden)[0].astype(jnp.bfloat16)
    grad_b_first = jnp.sum(grad_pre, axis=0, dtype=jnp.float32)
    grad_w_first = jnp.einsum("rd,rf->df", ffn_rows, grad_pre, preferred_element_type=jnp.float32)
    back_rows = jnp.einsum("rf,df->rd", grad_pre, w_first, preferred_element_type=jnp.float32)
    ffn_back = lax.psum_scatter(
        back_rows.reshape(seq_len, tables, model_width).astype(jnp.bfloat16),
        "mp",
        scatter_dimension=0,
        tiled=True,
    ).astype(jnp.float32)
    grad_second, gain_two, shift_two = normalize_back(
        grad_third + ffn_back, second_unit, second_inv, norm_gain[1]
    )
    bias_two = jnp.sum(grad_second, axis=(0, 1))
    gathered_cross_grad = lax.all_gather(grad_second.astype(jnp.bfloat16), "mp", axis=0, tiled=True)
    grad_cross_out = jnp.einsum(
        "lbh,lbd->hd", cross_mixed, gathered_cross_grad, preferred_element_type=jnp.float32
    )
    cross_mixed_grad = jnp.einsum(
        "lbd,hd->lbh", gathered_cross_grad, cross_out, preferred_element_type=jnp.float32
    ).astype(jnp.bfloat16)
    cq_grad, ck_grad, cv_grad = attend_back(
        split_heads(cross_query),
        split_heads(cross_key),
        split_heads(cross_value),
        cross_allowed,
        cross_lse,
        split_heads(cross_mixed_grad),
        scale_factor,
    )
    cq_low = join_heads(cq_grad).astype(jnp.bfloat16)
    kv_low = jnp.stack([join_heads(ck_grad), join_heads(cv_grad)], axis=2).astype(jnp.bfloat16)
    grad_cross_q = jnp.einsum(
        "lbd,lbh->dh", gathered_first, cq_low, preferred_element_type=jnp.float32
    )
    grad_cross_kv = jnp.einsum(
        "mbd,mbch->dch", gathered_memory, kv_low, preferred_element_type=jnp.float32
    )
    grad_cross_qv = jnp.stack(
        [
            jnp.sum(cq_low, axis=(0, 1), dtype=jnp.float32),
            jnp.sum(kv_low[:, :, 1], axis=(0, 1), dtype=jnp.float32),
        ]
    )
    first_part = jnp.einsum("lbh,dh->lbd", cq_low, cross_q, preferred_element_type=jnp.float32)
    memory_part = jnp.einsum("mbch,dch->mbd", kv_low, cross_kv, preferred_element_type=jnp.float32)
    first_back, memory_back = (
        lax.psum_scatter(
            first_part.astype(jnp.bfloat16), "mp", scatter_dimension=0, tiled=True
        ).astype(jnp.float32),
        lax.psum_scatter(
            memory_part.astype(jnp.bfloat16), "mp", scatter_dimension=0, tiled=True
        ).astype(jnp.float32),
    )
    grad_first, gain_one, shift_one = normalize_back(
        grad_second + first_back, first_unit, first_inv, norm_gain[0]
    )
    bias_one = jnp.sum(grad_first, axis=(0, 1))
    gathered_self_grad = lax.all_gather(grad_first.astype(jnp.bfloat16), "mp", axis=0, tiled=True)
    grad_self_out = jnp.einsum(
        "lbh,lbd->hd", self_mixed, gathered_self_grad, preferred_element_type=jnp.float32
    )
    self_mixed_grad = jnp.einsum(
        "lbd,hd->lbh", gathered_self_grad, self_out, preferred_element_type=jnp.float32
    ).astype(jnp.bfloat16)
    sq_grad, sk_grad, sv_grad = attend_back(
        split_heads(self_query),
        split_heads(self_key),
        split_heads(self_value),
        self_allowed,
        self_lse,
        split_heads(self_mixed_grad),
        scale_factor,
    )
    qkv_low = jnp.stack(
        [join_heads(sq_grad), join_heads(sk_grad), join_heads(sv_grad)], axis=2
    ).astype(jnp.bfloat16)
    grad_self_qkv = jnp.einsum(
        "lbd,lbch->dch", gathered_tags, qkv_low, preferred_element_type=jnp.float32
    )
    grad_self_qv = jnp.sum(qkv_low[:, :, 0::2], axis=(0, 1), dtype=jnp.float32)
    tag_part = jnp.einsum("lbch,dch->lbd", qkv_low, self_qkv, preferred_element_type=jnp.float32)
    shared = jnp.stack(
        [
            bias_one,
            bias_two,
            bias_three,
            gain_one,
            gain_two,
            gain_three,
            shift_one,
            shift_two,
            shift_three,
        ]
    )
    tag_back, shared_part = (
        lax.psum_scatter(
            tag_part.astype(jnp.bfloat16), "mp", scatter_dimension=0, tiled=True
        ).astype(jnp.float32),
        lax.psum_scatter(shared.astype(jnp.bfloat16), "mp", scatter_dimension=1, tiled=True).astype(
            jnp.float32
        ),
    )
    tags_grad = (grad_first + tag_back).astype(jnp.bfloat16)
    summed = (
        lax.psum(grad_self_qkv.astype(jnp.bfloat16), "dp").astype(jnp.float32),
        lax.psum(grad_self_qv.astype(jnp.bfloat16), "dp").astype(jnp.float32),
        lax.psum(grad_self_out.astype(jnp.bfloat16), "dp").astype(jnp.float32),
        lax.psum(grad_cross_q.astype(jnp.bfloat16), "dp").astype(jnp.float32),
        lax.psum(grad_cross_kv.astype(jnp.bfloat16), "dp").astype(jnp.float32),
        lax.psum(grad_cross_qv.astype(jnp.bfloat16), "dp").astype(jnp.float32),
        lax.psum(grad_cross_out.astype(jnp.bfloat16), "dp").astype(jnp.float32),
        lax.psum(grad_w_first.astype(jnp.bfloat16), "dp").astype(jnp.float32),
        lax.psum(grad_b_first.astype(jnp.bfloat16), "dp").astype(jnp.float32),
        lax.psum(grad_w_second.astype(jnp.bfloat16), "dp").astype(jnp.float32),
        lax.psum(shared_part.astype(jnp.bfloat16), "dp").astype(jnp.float32),
    )
    shared_total = summed[10]
    return (
        result.astype(jnp.bfloat16),
        tags_grad,
        memory_back.astype(jnp.bfloat16),
        summed[0],
        summed[1],
        summed[2],
        summed[3],
        summed[4],
        summed[5],
        summed[6],
        summed[7],
        summed[8],
        summed[9],
        shared_total[0:3],
        shared_total[3:6],
        shared_total[6:9],
    )


def solution(mesh):
    return jax.shard_map(
        per_device,
        mesh=mesh,
        in_specs=(
            P("mp", "dp", None),
            P("mp", "dp", None),
            P("mp", "dp", None),
            P("dp"),
            P("dp"),
            P(None, None, "mp"),
            P(None, "mp"),
            P("mp", None),
            P(None, "mp"),
            P(None, None, "mp"),
            P(None, "mp"),
            P("mp", None),
            P(None, "mp"),
            P("mp"),
            P("mp", None),
            P(),
            P(),
            P(),
        ),
        out_specs=(
            P("mp", "dp", None),
            P("mp", "dp", None),
            P("mp", "dp", None),
            P(None, None, "mp"),
            P(None, "mp"),
            P("mp", None),
            P(None, "mp"),
            P(None, None, "mp"),
            P(None, "mp"),
            P("mp", None),
            P(None, "mp"),
            P("mp"),
            P("mp", None),
            P(None, "mp"),
            P(None, "mp"),
            P(None, "mp"),
        ),
        check_vma=False,
    )
```

profile of v0, /device:TPU:0, one launch (start us, length us, event | category | flops | bytes accessed | tf_op | source)
XLA Modules:
  0.0 974.4 jit_solution(14609527220458912744)
XLA Ops:
  10.8 28.7 %all-gather.8.cloned.1.call-done = bf16[512,4,512]{2,0,1:T(8,128)(2,1)} async-done(((bf16[128,4,512]{2,0,1:T(8,128)(2,1)}), bf16[512,4,512]{2,0,1:T(8,128)(2,1)}) %all-gather.8.cloned.1.call-update) | async-done | bytes 2097168 | tf_op jit(solution)/shard_map/all_gather | solution.py:109
  51.9 35.3 %reduce-scatter.10.cloned.1.call-done = bf16[128,4,512]{2,0,1:T(8,128)(2,1)} async-done(((bf16[512,4,512]{2,0,1:T(8,128)(2,1)}), bf16[128,4,512]{2,0,1:T(8,128)(2,1)}) %reduce-scatter.10.cloned.1.call-update) | async-done | bytes 524304 | tf_op jit(solution)/shard_map/reduce_scatter | solution.py:134
  91.3 30.1 %all-gather.10.cloned.1.call-done = bf16[784,4,512]{2,1,0:T(4,128)(2,1)} async-done(((bf16[196,4,512]{2,1,0:T(4,128)(2,1)}), bf16[784,4,512]{2,1,0:T(4,128)(2,1)}) %all-gather.10.cloned.1.call-update) | async-done | bytes 3211280 | tf_op jit(solution)/shard_map/all_gather | solution.py:110
  121.3 4.8 fusion.7
  126.1 23.5 %all-gather.12.cloned.1.call-done = bf16[512,4,512]{2,0,1:T(8,128)(2,1)} async-done(((bf16[128,4,512]{2,0,1:T(8,128)(2,1)}), bf16[512,4,512]{2,0,1:T(8,128)(2,1)}) %all-gather.12.cloned.1.call-update) | async-done | bytes 2097168 | tf_op jit(solution)/shard_map/all_gather | solution.py:140
  164.4 37.3 %reduce-scatter.12.cloned.1.call-done = bf16[128,4,512]{2,0,1:T(8,128)(2,1)} async-done(((bf16[512,4,512]{2,0,1:T(8,128)(2,1)}), bf16[128,4,512]{2,0,1:T(8,128)(2,1)}) %reduce-scatter.12.cloned.1.call-update) | async-done | bytes 524304 | tf_op jit(solution)/shard_map/reduce_scatter | solution.py:161
  205.3 25.5 %all-gather.14.cloned.1.call-done = bf16[512,4,512]{2,0,1:T(8,128)(2,1)} async-done(((bf16[128,4,512]{2,0,1:T(8,128)(2,1)}), bf16[512,4,512]{2,0,1:T(8,128)(2,1)}) %all-gather.14.cloned.1.call-update) | async-done | bytes 2097168 | tf_op jit(solution)/shard_map/all_gather | solution.py:168
  230.7 4.6 copy.98
  243.3 4.0 convert_element_type.428
  250.6 37.8 %reduce-scatter.14.cloned.1.call-done = bf16[128,4,512]{2,0,1:T(8,128)(2,1)} async-done(((bf16[512,4,512]{2,0,1:T(8,128)(2,1)}), bf16[128,4,512]{2,0,1:T(8,128)(2,1)}) %reduce-scatter.14.cloned.1.call-update) | async-done | bytes 524304 | tf_op jit(solution)/shard_map/reduce_scatter | solution.py:174
  293.9 26.1 %all-gather.16.cloned.1.call-done = bf16[512,4,512]{2,0,1:T(8,128)(2,1)} async-done(((bf16[128,4,512]{2,0,1:T(8,128)(2,1)}), bf16[512,4,512]{2,0,1:T(8,128)(2,1)}) %all-gather.16.cloned.1.call-update) | async-done | bytes 2097168 | tf_op jit(solution)/shard_map/all_gather | solution.py:188
  320.0 4.6 copy.101
  328.5 4.6 fusion.120
  343.7 37.6 %reduce-scatter.16.cloned.1.call-done = bf16[128,4,512]{2,0,1:T(8,128)(2,1)} async-done(((bf16[512,4,512]{2,0,1:T(8,128)(2,1)}), bf16[128,4,512]{2,0,1:T(8,128)(2,1)}) %reduce-scatter.16.cloned.1.call-update) | async-done | bytes 524304 | tf_op jit(solution)/shard_map/reduce_scatter | solution.py:195
  387.0 25.3 %all-gather.18.cloned.1.call-done = bf16[512,4,512]{2,0,1:T(8,128)(2,1)} async-done(((bf16[128,4,512]{2,0,1:T(8,128)(2,1)}), bf16[512,4,512]{2,0,1:T(8,128)(2,1)}) %all-gather.18.cloned.1.call-update) | async-done | bytes 2097168 | tf_op jit(solution)/shard_map/all_gather | solution.py:205
  414.9 4.9 multiply_reduce_fusion
  430.0 37.8 %reduce-scatter.18.cloned.1.call-done = bf16[128,4,512]{2,0,1:T(8,128)(2,1)} async-done(((bf16[512,4,512]{2,0,1:T(8,128)(2,1)}), bf16[128,4,512]{2,0,1:T(8,128)(2,1)}) %reduce-scatter.18.cloned.1.call-update) | async-done | bytes 524304 | tf_op jit(solution)/shard_map/reduce_scatter | solution.py:238
  477.4 4.3 fusion.131
  483.6 4.2 copy.112
  521.5 57.8 %all-reduce.6.cloned.1.call-done = bf16[784,4,512]{2,1,0:T(4,128)(2,1)} async-done(((bf16[784,4,512]{2,1,0:T(4,128)(2,1)}), bf16[784,4,512]{2,1,0:T(4,128)(2,1)}) %all-reduce.6.cloned.1.call-update) | async-done | bytes 3211280
  581.6 26.5 %reduce-scatter.22.cloned.1.call-done = bf16[128,9]{1,0:T(8,128)(2,1)} async-done(((bf16[512,9]{1,0:T(8,128)(2,1)}), bf16[128,9]{1,0:T(8,128)(2,1)}) %reduce-scatter.22.cloned.1.call-update) | async-done | bytes 2320
  609.6 82.9 %all-reduce.1 = (bf16[9,128]{1,0:T(8,128)(2,1)S(1)}, bf16[2,128]{1,0:T(2,128)(2,1)S(1)}, bf16[2,128]{1,0:T(2,128)(2,1)S(1)}, bf16[256]{0:T(256)(128)(2,1)S(1)}) all-reduce(bf16[9,128]{1,0:T(8,128)(2,1)S(1)} %copy.145, bf16[2,128]{1,0:T(2,128)(2,1)S(1)} %slice_reduce_fusion, ...), channel_id=1, replica_groups=mesh['dp'=32,'mp'=4] {'dp'}, use_global_device_ids=true, to_apply=%region_49.50 | all-reduce | flops 1920 | bytes 7680 | tf_op jit(solution)/shard_map/psum | solution.py:306
  694.8 229.3 %all-reduce.8.cloned.1.call-done = (bf16[512,3,128]{0,2,1:T(8,128)(2,1)}, bf16[512,2,128]{0,2,1:T(8,128)(2,1)}, bf16[128,512]{1,0:T(8,128)(2,1)}, bf16[512,128]{...) async-done(((bf16[512,3,128]{0,2,1:T(8,128)(2,1)}, bf16[512,2,128]{0,2,1:T(8,128)(2,1)}, ...) | async-done | bytes 1572880 | tf_op jit(solution)/shard_map/psum | solution.py:296
  933.7 31.3 %reduce-scatter.20.cloned.1.call-done = bf16[128,4,512]{2,0,1:T(8,128)(2,1)} async-done(((bf16[512,4,512]{2,0,1:T(8,128)(2,1)}), bf16[128,4,512]{2,0,1:T(8,128)(2,1)}) %reduce-scatter.20.cloned.1.call-update) | async-done | bytes 524304 | tf_op jit(solution)/shard_map/reduce_scatter | solution.py:287
  (324 shorter events, 149.7 us)
Async XLA Ops:
  7.2 32.4 %all-gather.8.cloned.1.call-start = ((), (), s32[]{:S(2)}) async-start(), calls=%async_computation.7 | async-start | bytes 2621440 | tf_op jit(solution)/shard_map/all_gather | solution.py:109
  9.2 78.0 %reduce-scatter.10.cloned.1.call-start = ((), (), s32[]{:S(2)}) async-start(), calls=%async_computation.8 | async-start | bytes 2621440 | tf_op jit(solution)/shard_map/reduce_scatter | solution.py:134
  49.4 72.0 %all-gather.10.cloned.1.call-start = ((), (), s32[]{:S(2)}) async-start(), calls=%async_computation.9 | async-start | bytes 4014080 | tf_op jit(solution)/shard_map/all_gather | solution.py:110
  50.1 99.4 %all-gather.12.cloned.1.call-start = ((), (), s32[]{:S(2)}) async-start(), calls=%async_computation.10 | async-start | bytes 2621440 | tf_op jit(solution)/shard_map/all_gather | solution.py:140
  51.4 150.3 %copy-start.53 = (f32[1,512]{1,0:T(1,128)}, f32[1,512]{1,0:T(1,128)S(1)}, u32[]{:S(2)}) copy-start(f32[1,512]{1,0:T(1,128)S(1)} %get-tuple-element.105) | copy-start | bytes 6148
  51.4 152.2 %copy-start.54 = (f32[1,512]{1,0:T(1,128)}, f32[1,512]{1,0:T(1,128)S(1)}, u32[]{:S(2)}) copy-start(f32[1,512]{1,0:T(1,128)S(1)} %get-tuple-element.106) | copy-start | bytes 6148
  51.9 151.6 %copy-start.61 = (f32[1,512]{1,0:T(1,128)}, f32[1,512]{1,0:T(1,128)S(1)}, u32[]{:S(2)}) copy-start(f32[1,512]{1,0:T(1,128)S(1)} %get-tuple-element.109) | copy-start | bytes 6148
  90.0 111.7 %copy-start.52 = (f32[128,4]{0,1:T(4,128)}, f32[128,4]{0,1:T(4,128)S(1)}, u32[]{:S(2)}) copy-start(f32[128,4]{0,1:T(4,128)S(1)} %add_rsqrt_fusion.2) | copy-start | bytes 6148
  91.1 110.6 %reduce-scatter.12.cloned.1.call-start = ((), (), s32[]{:S(2)}) async-start(), calls=%async_computation.11 | async-start | bytes 2621440 | tf_op jit(solution)/shard_map/reduce_scatter | solution.py:161
  91.2 65.1 %copy-start.76 = (f32[128]{0:T(128)}, f32[128]{0:T(128)S(1)}, u32[]{:S(2)}) copy-start(f32[128]{0:T(128)S(1)} %get-tuple-element.113) | copy-start | bytes 1540
  163.9 66.9 %all-gather.14.cloned.1.call-start = ((), (), s32[]{:S(2)}) async-start(), calls=%async_computation.12 | async-start | bytes 2621440 | tf_op jit(solution)/shard_map/all_gather | solution.py:168
  204.6 83.8 %reduce-scatter.14.cloned.1.call-start = ((), (), s32[]{:S(2)}) async-start(), calls=%async_computation.13 | async-start | bytes 2621440 | tf_op jit(solution)/shard_map/reduce_scatter | solution.py:174
  250.6 69.4 %all-gather.16.cloned.1.call-start = ((), (), s32[]{:S(2)}) async-start(), calls=%async_computation.14 | async-start | bytes 2621440 | tf_op jit(solution)/shard_map/all_gather | solution.py:188
  293.9 87.5 %reduce-scatter.16.cloned.1.call-start = ((), (), s32[]{:S(2)}) async-start(), calls=%async_computation.15 | async-start | bytes 2621440 | tf_op jit(solution)/shard_map/reduce_scatter | solution.py:195
  343.5 68.9 %all-gather.18.cloned.1.call-start = ((), (), s32[]{:S(2)}) async-start(), calls=%async_computation.16 | async-start | bytes 2621440 | tf_op jit(solution)/shard_map/all_gather | solution.py:205
  386.3 81.6 %reduce-scatter.18.cloned.1.call-start = ((), (), s32[]{:S(2)}) async-start(), calls=%async_computation.17 | async-start | bytes 2621440 | tf_op jit(solution)/shard_map/reduce_scatter | solution.py:238
  427.9 39.9 %copy-start.5 = (bf16[128,4,512]{2,1,0:T(4,128)(2,1)S(1)}, bf16[128,4,512]{2,1,0:T(4,128)(2,1)}, u32[]{:S(2)}) copy-start(bf16[128,4,512]{2,1,0:T(4,128)(2,1)} %param.18) | copy-start | bytes 1572868
  427.9 39.9 %copy-start.8 = (bf16[128,4,512]{2,0,1:T(8,128)(2,1)S(1)}, bf16[128,4,512]{2,0,1:T(8,128)(2,1)}, u32[]{:S(2)}) copy-start(bf16[128,4,512]{2,0,1:T(8,128)(2,1)} %reduce-scatter.10.cloned.1.call-done) | copy-start | bytes 1572868
  430.0 72.1 %all-gather.20.cloned.1.call-start = ((), (), s32[]{:S(2)}) async-start(), calls=%async_computation.18 | async-start | bytes 2621440 | tf_op jit(solution)/shard_map/all_gather | solution.py:249
  474.2 105.0 %all-reduce.6.cloned.1.call-start = ((), (), s32[]{:S(2)}) async-start(), calls=%async_computation.21 | async-start | bytes 6422528
  487.8 120.2 %reduce-scatter.22.cloned.1.call-start = ((), (), s32[]{:S(2)}) async-start(), calls=%async_computation.20 | async-start | bytes 163840
  501.8 422.2 %all-reduce.8.cloned.1.call-start = ((), (), s32[]{:S(2)}) async-start(), calls=%async_computation.22 | async-start | bytes 3145728 | tf_op jit(solution)/shard_map/psum | solution.py:296
  515.6 449.5 %reduce-scatter.20.cloned.1.call-start = ((), (), s32[]{:S(2)}) async-start(), calls=%async_computation.19 | async-start | bytes 2621440 | tf_op jit(solution)/shard_map/reduce_scatter | solution.py:287
  925.7 39.3 %copy-start.12 = (f32[128,4,512]{2,0,1:T(8,128)S(1)}, f32[128,4,512]{2,0,1:T(8,128)}, u32[]{:S(2)}) copy-start(f32[128,4,512]{2,0,1:T(8,128)} %copy-done.11) | copy-start | bytes 3145732
  (83 other events, 450.2 us)
Sparse Core Ops, SparseCore 0:
  10.3 29.2 all-gather.7
  49.5 37.6 reduce-scatter.9
  89.0 32.2 all-gather.9
  123.5 25.9 all-gather.11
  164.0 37.6 reduce-scatter.11
  204.8 25.9 all-gather.13
  250.7 37.6 reduce-scatter.13
  294.0 25.9 all-gather.15
  343.6 37.6 reduce-scatter.15
  386.4 25.9 all-gather.17
  430.1 37.6 reduce-scatter.17
  474.3 25.9 all-gather.19
  503.0 76.2 all-reduce.5
  582.2 25.8 reduce-scatter.21
  612.4 311.5 all-reduce.7
  926.5 38.5 reduce-scatter.19
where the time goes:
time: 984 us; the launch traced here: 974 us
  waiting for transfers between devices  691 us (70%)
  blocking collectives  82.9 us (8%)
  matrix products  77.2 us (8%)
  local copies, waits for them, and re-layouts  62.3 us (6%)
  other arithmetic  43.4 us (4%)
  between operations  16 us (2%)
    psum x1, waiting for transfers between devices, per_device(): lax.psum(grad_self_qkv.astype(jnp.bfloat16), 'dp').astype(jnp.float32)  229 us
    unnamed x18, waiting for transfers between devices  85.3 us
    psum x1, blocking collectives, per_device(): lax.psum(shared_part.astype(jnp.bfloat16), 'dp').astype(jnp.float32)  82.9 us
    reduce_scatter x1, waiting for transfers between devices, per_device(): lax.psum_scatter(first_part.astype(jnp.bfloat16), 'mp', scatter_dimension...  37.8 us
    reduce_scatter x1, waiting for transfers between devices, per_device(): lax.psum_scatter(ffn_rows_out.reshape(seq_len, tables, model_width).astyp...  37.8 us
    reduce_scatter x1, waiting for transfers between devices, per_device(): lax.psum_scatter(back_rows.reshape(seq_len, tables, model_width).astype(j...  37.6 us
    reduce_scatter x1, waiting for transfers between devices, per_device(): lax.psum_scatter(cross_term.astype(jnp.bfloat16), 'mp', scatter_dimension...  37.3 us
    reduce_scatter x1, waiting for transfers between devices, per_device(): lax.psum_scatter(self_term.astype(jnp.bfloat16), 'mp', scatter_dimension=...  35.3 us
  transfers between devices with their start and end apart: 16, of which 15 were waited for; matrix products, arithmetic and copies ran while one was open for 7% of the time, Pallas kernels for 0%

commit v1 on v0

v1 whole, which is shorter than its diff:
```python
import math

import jax
import jax.numpy as jnp
from jax import lax
from jax.experimental import pallas as pl
from jax.experimental.pallas import tpu as pltpu
from jax.sharding import PartitionSpec as P

BF = jnp.bfloat16
F32 = jnp.float32
D = 512
HEADS = 4
HEAD = 128
L = 512
MLOC = 196
MPAD = 208
MT = 4 * MPAD
QB = 256
EPSILON = 1e-05
SCALE = 1.0 / math.sqrt(HEAD)
LOG2E = math.log2(math.e)
NEG = -1e30


def mm(a, b):
    return jnp.dot(a, b, preferred_element_type=F32)


def mm_nt(a, b):
    return lax.dot_general(a, b, (((1,), (1,)), ((), ())), preferred_element_type=F32)


def mm_tn(a, b):
    return lax.dot_general(a, b, (((0,), (0,)), ((), ())), preferred_element_type=F32)


def col_weight(w, unit):
    return jnp.concatenate([w[s, unit] for s in range(4)], axis=1)


def row_block(w, s, unit):
    return jnp.concatenate([w[s, unit, pl.ds(j * 128, 128), :] for j in range(4)], axis=1)


def row_weight(w, unit):
    return jnp.concatenate([row_block(w, s, unit) for s in range(4)], axis=0)


def put_cols(g, unit, value):
    for s in range(4):
        g[s // 2, s % 2, unit] = value[:, s * 128 : (s + 1) * 128].astype(BF)


def put_rows(g, s, unit, value):
    for j in range(4):
        g[s // 2, s % 2, unit, pl.ds(j * 128, 128), :] = value[:, j * 128 : (j + 1) * 128].astype(BF)


def norm_rows(v):
    center = v - jnp.mean(v, axis=-1, keepdims=True)
    inverse = lax.rsqrt(jnp.mean(center * center, axis=-1, keepdims=True) + EPSILON)
    return center * inverse, inverse


def norm_back(e, unit, inverse, gain):
    scaled = e * gain
    return inverse * (
        scaled
        - jnp.mean(scaled, axis=-1, keepdims=True)
        - unit * jnp.mean(scaled * unit, axis=-1, keepdims=True)
    )


def norm_back_rows(r, n, e, unit, inverse):
    gain = r.pvec[pl.ds(3 + n, 1), :]
    totals = [jnp.zeros((8, D), F32)] * 3
    for i in range(L // 128):
        rows = slice(i * 128, (i + 1) * 128)
        ei, ui = e[rows, :].astype(F32), unit[rows, :]
        di = norm_back(ei, ui, inverse[rows, :], gain)
        yield rows, di
        parts = (di, ei * ui, ei)
        totals = [t + jnp.sum(v.reshape(16, 8, D), axis=0) for t, v in zip(totals, parts)]
    for j in range(3):
        r.sums[pl.ds(3 * j + n, 1), :] = jnp.sum(totals[j], axis=0, keepdims=True)


GELU_C = math.sqrt(2.0 / math.pi)


def gelu_both(z):
    z2 = z * z
    t = jnp.tanh(GELU_C * z * (1.0 + 0.044715 * z2))
    half = 0.5 * (1.0 + t)
    return z * half, half + (0.5 * GELU_C) * z * (1.0 - t * t) * (1.0 + 3 * 0.044715 * z2)


def col_sum(v):
    return jnp.sum(v, axis=0, keepdims=True)


def bias_row(small, row):
    return jnp.concatenate([small[s, pl.ds(row, 1), :] for s in range(4)], axis=1)


def head_rows(h):
    return pl.ds(h * HEAD if isinstance(h, int) else pl.multiple_of(h * HEAD, HEAD), HEAD)


def attend(q, k, v, p, ot, rinv, sbuf, keybias, causal, limit, key_block, heads):
    items = [(h, qb) for h in heads for qb in range(L // QB)]
    peaks, totals = {}, {}

    def score(i, kb):
        h, qb = items[i]
        rows = pl.ds(kb * key_block, key_block)
        s = mm_nt(k[h, rows, :], q[h, pl.ds(qb * QB, QB), :])
        s = s + jnp.concatenate([keybias[rows, :]] * (QB // 128), axis=1)
        if causal and kb == qb:
            key = lax.broadcasted_iota(jnp.int32, s.shape, 0)
            query = lax.broadcasted_iota(jnp.int32, s.shape, 1)
            s = jnp.where(key <= query, s, NEG)
        sbuf[i % 2, rows, :] = s
        top = jnp.max(s, axis=0, keepdims=True)
        peaks[i] = jnp.maximum(peaks[i], top) if kb else top

    def weigh(i, kb):
        h, qb = items[i]
        rows = pl.ds(kb * key_block, key_block)
        e = jnp.exp2(sbuf[i % 2, rows, :] * (SCALE * LOG2E) - peaks[i] * (SCALE * LOG2E))
        p[h, rows, pl.ds(qb * QB, QB)] = e.astype(BF)
        part = jnp.sum(e, axis=0, keepdims=True)
        totals[i] = totals[i] + part if kb else part

    def output(i):
        h, qb = items[i]
        cols, keys = pl.ds(qb * QB, QB), limit(qb)
        inv = 1.0 / totals[i]
        rinv[h, :, cols] = jnp.broadcast_to(inv, (8, QB))
        o = mm(v[h, pl.ds(0, keys), :].T, p[h, pl.ds(0, keys), cols])
        ot[head_rows(h), cols] = (o * inv).astype(BF)

    blocks = [limit(qb) // key_block for _, qb in items]
    for i in range(len(items) + 2):
        ahead = blocks[i] if i < len(items) else 0
        behind = blocks[i - 1] if 0 < i <= len(items) else 0
        for kb in range(max(ahead, behind)):
            if kb < ahead:
                score(i, kb)
            if kb < behind:
                weigh(i - 1, kb)
        if i > 1:
            output(i - 2)


def scaled_heads(do, grad, rinv):
    for h in range(HEADS):
        inv = rinv[h].T[:, :1]
        do[h] = (grad[:, h * HEAD : (h + 1) * HEAD] * inv).astype(BF)


def attend_grad(q, k, v, p, ot, do, dqt, dk, dsbuf, limit, key_block, pair):
    def one(h):
        kt = k[h].T
        span = head_rows(h)
        delta = jnp.sum(ot[span, :].astype(F32) * do[h].T.astype(F32), axis=0, keepdims=True)
        for qb in range(L // QB):
            cols = pl.ds(qb * QB, QB)
            keys = limit(qb)
            dov = do[h, cols, :]
            low = delta[:, qb * QB : (qb + 1) * QB]
            for kb in range(keys // key_block):
                rows = pl.ds(kb * key_block, key_block)
                dw = mm_nt(v[h, rows, :], dov)
                dsbuf[rows, cols] = (p[h, rows, cols].astype(F32) * (dw - low)).astype(BF)
            dq = mm(kt[:, :keys], dsbuf[pl.ds(0, keys), cols]) * SCALE
            dqt[span, cols] = dq.astype(BF)
        for rows, seen in seen_blocks(limit):
            dk[h, rows, :] = (mm(dsbuf[rows, seen], q[h, seen, :]) * SCALE).astype(BF)

    one(2 * pair)
    one(2 * pair + 1)


def seen_blocks(limit):
    below = 0
    for qb in range(L // QB):
        keys = limit(qb) - below
        if keys:
            yield pl.ds(below, keys), pl.ds(qb * QB, L - qb * QB)
        below = limit(qb)


def value_grad(p, do, dv, limit):
    def one(h):
        for rows, seen in seen_blocks(limit):
            dv[h, rows, :] = mm(p[h, rows, seen], do[h, seen, :]).astype(BF)

    for h in range(HEADS):
        one(h)


def scratch_list():
    v = pltpu.VMEM
    return dict(
        q=v((4, L, HEAD), BF), k=v((4, L, HEAD), BF), v=v((4, L, HEAD), BF),
        ps=v((4, L, L), BF), ots=v((D, L), BF), rs=v((4, 8, L), F32),
        h1=v((L, D), F32), h1b=v((L, D), BF), u1=v((L, D), F32), inv1=v((L, 1), F32),
        qc=v((4, L, HEAD), BF), kc=v((4, MT, HEAD), BF), vc=v((4, MT, HEAD), BF),
        pc=v((4, MT, L), BF), otc=v((D, L), BF), rc=v((4, 8, L), F32),
        h2b=v((L, D), BF), g=v((L, 2 * D), BF), dfb=v((L, D), BF), dz=v((L, 2 * D), BF),
        dr2=v((L, D), F32), da2=v((L, D), BF), doc=v((4, L, HEAD), BF),
        dkc=v((4, MT, HEAD), BF), dvc=v((4, MT, HEAD), BF), dqc=v((L, D), BF),
        sbuf=v((2, MT, QB), F32), dsbuf=v((MT, L), BF), keybias=v((MT, 128), F32),
    )


class Refs:
    def __init__(self, **kw):
        self.__dict__.update(kw)
        self.ob = self.dq = self.dqc
        self.xt = self.h2b
        self.dqt, self.dr1 = self.otc, self.h1
        self.da1, self.dos = self.da2, self.doc
        self.dk, self.dv = self.qc, self.vc.at[:, pl.ds(0, L), :]
        self.tgrad, self.mgrad = self.cot_t, self.mem_t


def stage_qkv(r, pair):
    heads = (2 * pair, 2 * pair + 1)
    for j, (dst, row) in enumerate(((r.q, 0), (r.k, None), (r.v, 1))):
        y = mm(r.x[...], jnp.concatenate([r.w[h, j] for h in heads], axis=1))
        if row is not None:
            y = y + jnp.concatenate([r.small[h, pl.ds(row, 1), :] for h in heads], axis=1)
        y = y.astype(BF)
        for i, h in enumerate(heads):
            dst[h] = y[:, i * HEAD : (i + 1) * HEAD]


def self_limit(qb):
    return (qb + 1) * QB


def stage_self_mask(r):
    key = lax.broadcasted_iota(jnp.int32, (L, 128), 0)
    r.keybias[pl.ds(0, L), :] = jnp.where(key < r.lens[pl.ds(lax.axis_index("mp"), 1), :], 0.0, NEG)


def stage_cross_mask(r):
    token = lax.broadcasted_iota(jnp.int32, (MPAD, 128), 0)
    memlen = r.lens[pl.ds(4 + lax.axis_index("mp"), 1), :]
    for i in range(4):
        seen = (token < MLOC) & (token + i * MLOC < memlen)
        r.keybias[pl.ds(i * MPAD, MPAD), :] = jnp.where(seen, 0.0, NEG)


def stage_self(r, pair):
    heads = (2 * pair, 2 * pair + 1)
    attend(r.q, r.k, r.v, r.ps, r.ots, r.rs, r.sbuf, r.keybias, True, self_limit, QB, heads)


def stage_first(r):
    r.ob[...] = r.ots[...].T
    wso = row_weight(r.w, 3)

    rows = pl.ds(0, L)
    v = r.x[rows, :].astype(F32) + mm(r.ob[rows, :], wso) + r.pvec[pl.ds(0, 1), :]
    unit, inv = norm_rows(v)
    r.u1[rows, :] = unit
    r.inv1[rows, :] = inv
    h1 = unit * r.pvec[pl.ds(3, 1), :] + r.pvec[pl.ds(6, 1), :]
    r.h1[rows, :] = h1
    r.h1b[rows, :] = h1.astype(BF)


def stage_cross_q(r):
    y = (mm(r.h1b[...], col_weight(r.w, 4)) + bias_row(r.small, 2)).astype(BF)
    for h in range(HEADS):
        r.qc[h] = y[:, h * HEAD : (h + 1) * HEAD]


def stage_cross_kv(r):
    for j, (dst, row) in enumerate(((r.kc, None), (r.vc, 3))):
        y = mm(r.m[...], col_weight(r.w, 5 + j))
        if row is not None:
            y = y + bias_row(r.small, row)
        y = y.astype(BF)
        for h in range(HEADS):
            dst[h] = y[:, h * HEAD : (h + 1) * HEAD]


def cross_limit(qb):
    return MT


def stage_cross(r):
    attend(r.qc, r.kc, r.vc, r.pc, r.otc, r.rc, r.sbuf, r.keybias, False, cross_limit, MPAD, range(HEADS))


def ffn_weights(r, s):
    w_in = jnp.concatenate([r.w[s, 8], r.w[s, 9]], axis=1)
    w_out = jnp.concatenate([row_block(r.w, s, 10), row_block(r.w, s, 11)], axis=0)
    return w_in, w_out


def stage_rows(r, cotangent_ready=lambda: None):
    r.ob[...] = r.otc[...].T

    v = r.h1[...] + mm(r.ob[...], row_weight(r.w, 7)) + r.pvec[pl.ds(1, 1), :]
    u2, inv2 = norm_rows(v)
    h2 = u2 * r.pvec[pl.ds(4, 1), :] + r.pvec[pl.ds(7, 1), :]
    h2b = h2.astype(BF)
    r.h2b[...] = h2b
    r3 = h2 + r.pvec[pl.ds(2, 1), :]
    slopes = []
    for s in range(4):
        w_in, w_out = ffn_weights(r, s)
        bias = jnp.concatenate([r.small[s, pl.ds(4, 1), :], r.small[s, pl.ds(5, 1), :]], axis=1)
        value, slope = gelu_both(mm(h2b, w_in) + bias)
        value = value.astype(BF)
        r.g[:, pl.ds(s * 256, 256)] = value
        slopes.append(slope)
        r3 = r3 + mm(value, w_out)
    u3, inv3 = norm_rows(r3)
    value = (u3 * r.pvec[pl.ds(5, 1), :] + r.pvec[pl.ds(8, 1), :]).astype(BF)
    for i in range(4):
        r.result[i] = value[i * 128 : (i + 1) * 128, :]
    cotangent_ready()
    r.dr2[...] = u2
    for rows, dr3 in norm_back_rows(r, 2, r.cot, u3, inv3):
        r.dr1[rows, :] = dr3
        r.dfb[rows, :] = dr3.astype(BF)
    return inv2, slopes


def stage_rows_back(r, kept):
    inv2, slopes = kept
    e2 = r.dr1[...]
    for s in range(4):
        w_in, w_out = ffn_weights(r, s)
        dz = (mm_nt(r.dfb[...], w_out) * slopes[s]).astype(BF)
        r.dz[:, pl.ds(s * 256, 256)] = dz
        e2 = e2 + mm_nt(dz, w_in)
    for rows, dr2 in norm_back_rows(r, 1, e2, r.dr2, inv2):
        r.dr2[rows, :] = dr2
        r.da2[rows, :] = dr2.astype(BF)
    scaled_heads(r.doc, mm_nt(r.da2[...], row_weight(r.w, 7)), r.rc)


def stage_ffn_out_grads(r):
    gt = r.g[...].T
    for s in range(4):
        y = mm(gt[s * 256 : (s + 1) * 256, :], r.dfb[...])
        for i in range(2):
            put_rows(r.grads, s, 10 + i, y[i * 128 : (i + 1) * 128, :])


def stage_ffn_grads(r):
    h2t = r.h2b[...].T
    for s in range(4):
        y = mm(h2t, r.dz[:, pl.ds(s * 256, 256)])
        r.grads[s // 2, s % 2, 8] = y[:, :128].astype(BF)
        r.grads[s // 2, s % 2, 9] = y[:, 128:].astype(BF)
        b = col_sum(r.dz[:, pl.ds(s * 256, 256)].astype(F32))
        r.bsums[s, pl.ds(4, 1), :] = b[:, :128]
        r.bsums[s, pl.ds(5, 1), :] = b[:, 128:]


def stage_cross_out_grad(r):
    y = mm(r.otc[...], r.da2[...])
    for s in range(4):
        put_rows(r.grads, s, 7, y[s * 128 : (s + 1) * 128, :])


def stage_cross_values(r):
    value_grad(r.pc, r.doc, r.dvc, cross_limit)


def stage_cross_back(r, pair):
    attend_grad(r.qc, r.kc, r.vc, r.pc, r.otc, r.doc, r.dqt, r.dkc, r.dsbuf, cross_limit, MPAD, pair)


def stage_cross_value_grads(r):
    mt = r.m[...].T
    dv = jnp.concatenate([r.dvc[h] for h in range(HEADS)], axis=1)
    put_cols(r.grads, 6, mm(mt, dv))
    b = col_sum(dv.astype(F32))
    for h in range(HEADS):
        r.bsums[h, pl.ds(3, 1), :] = b[:, h * HEAD : (h + 1) * HEAD]


def stage_cross_grads(r):
    mt = r.m[...].T
    r.dqc[...] = r.dqt[...].T
    put_cols(r.grads, 4, mm(r.h1b[...].T, r.dqc[...]))
    put_cols(r.grads, 5, mm(mt, jnp.concatenate([r.dkc[h] for h in range(HEADS)], axis=1)))
    b = col_sum(r.dqc[...].astype(F32))
    for h in range(HEADS):
        r.bsums[h, pl.ds(2, 1), :] = b[:, h * HEAD : (h + 1) * HEAD]


def stage_memory_grad(r):
    w = jnp.concatenate([col_weight(r.w, 5), col_weight(r.w, 6)], axis=1)
    parts = [d[h] for d in (r.dkc, r.dvc) for h in range(HEADS)]
    r.mgrad[...] = mm_nt(jnp.concatenate(parts, axis=1), w).astype(BF)


def stage_first_back(r):
    e1 = r.dr2[...] + mm_nt(r.dqc[...], col_weight(r.w, 4))
    for rows, dr1 in norm_back_rows(r, 0, e1, r.u1, r.inv1):
        r.dr1[rows, :] = dr1
        r.da1[rows, :] = dr1.astype(BF)
    scaled_heads(r.dos, mm_nt(r.da1[...], row_weight(r.w, 3)), r.rs)


def stage_self_out_grad(r):
    y = mm(r.ots[...], r.da1[...])
    for s in range(4):
        put_rows(r.grads, s, 3, y[s * 128 : (s + 1) * 128, :])


def stage_self_back(r, pair):
    attend_grad(r.q, r.k, r.v, r.ps, r.ots, r.dos, r.dqt, r.dk, r.dsbuf, self_limit, QB, pair)


def stage_self_values(r):
    value_grad(r.ps, r.dos, r.dv, self_limit)
    r.xt[...] = r.x[...].T
    dv = jnp.concatenate([r.dv[h] for h in range(HEADS)], axis=1)
    put_cols(r.grads, 2, mm(r.xt[...], dv))
    b = col_sum(dv.astype(F32))
    for h in range(HEADS):
        r.bsums[h, pl.ds(1, 1), :] = b[:, h * HEAD : (h + 1) * HEAD]


def stage_self_grads(r, pair):
    cols = pl.ds(pair * 256, 256)
    dq = r.dqt[cols, :].T
    r.dq[:, cols] = dq
    y = mm(r.xt[...], jnp.concatenate([dq, r.dk[2 * pair], r.dk[2 * pair + 1]], axis=1))
    b = col_sum(dq.astype(F32))
    for i in range(2):
        for j in range(2):
            r.grads[pair, i, j] = y[:, j * 256 + i * 128 : j * 256 + (i + 1) * 128].astype(BF)
        r.bsums[2 * pair + i, pl.ds(0, 1), :] = b[:, i * 128 : (i + 1) * 128]


def stage_tags_grad(r):
    w = jnp.concatenate([col_weight(r.w, j) for j in range(3)], axis=1)
    parts = [r.dq[...]] + [d[h] for d in (r.dk, r.dv) for h in range(HEADS)]
    y = (r.dr1[...] + mm_nt(jnp.concatenate(parts, axis=1), w)).astype(BF)
    for i in range(4):
        r.tgrad[i] = y[i * 128 : (i + 1) * 128, :]


MESH = pl.DeviceIdType.MESH


class Place:
    def __init__(self):
        dp, mp = lax.axis_index("dp"), lax.axis_index("mp")
        self.mp = mp
        self.x = lax.rem(dp, 4)
        self.lo = lax.rem(lax.div(dp, 4), 2)
        self.y = lax.div(dp, 8)
        self.hi = lax.div(mp, 2)
        self.core = lax.rem(mp, 2)

    def device(self, x=None, y=None, lo=None, hi=None, core=None):
        x = self.x if x is None else x
        y = self.y if y is None else y
        lo = self.lo if lo is None else lo
        hi = self.hi if hi is None else hi
        core = self.core if core is None else core
        return (y * 8 + lo * 4 + x, hi * 2 + core)

    def owner(self, t):
        return self.device(lo=1 - self.lo, hi=t // 2, core=t % 2)

    def sibling(self):
        return self.device(core=1 - self.core)

    def across(self):
        return self.device(lo=1 - self.lo, hi=1 - self.hi)

    def x_at(self, n):
        return lax.rem(self.x + n, 4)

    def y_at(self, n):
        return lax.rem(self.y + n, 4)

    def along(self, axis, n):
        return self.device(x=self.x_at(n)) if axis == 0 else self.device(y=self.y_at(n))

    def at(self, axis, n=0):
        return self.x_at(n) if axis == 0 else self.y_at(n)

    def peers(self):
        out = [self.owner(t) for t in range(4)]
        out.append(self.sibling())
        out.append(self.device(hi=1 - self.hi))
        for axis in range(2):
            out += [self.along(axis, n) for n in (1, 2, 3)]
        return out


class Phase:
    def __init__(self, links, view):
        self.links, self.view, self.slot, self.device = links, view, links.used, None
        links.used += 1

    def send(self, src, dst, device):
        self.device = device
        pltpu.make_async_remote_copy(
            src_ref=src,
            dst_ref=dst,
            send_sem=self.links.send_sems.at[self.slot],
            recv_sem=self.links.recv_sems.at[self.slot],
            device_id=device,
            device_id_type=MESH,
        ).start()
        if self not in self.links.started:
            self.links.started.append(self)

    def whole(self):
        return pltpu.make_async_remote_copy(
            src_ref=self.view,
            dst_ref=self.view,
            send_sem=self.links.send_sems.at[self.slot],
            recv_sem=self.links.recv_sems.at[self.slot],
            device_id=self.device,
            device_id_type=MESH,
        )

    def wait(self):
        self.whole().wait_recv()

class Links:
    def __init__(self, send_sems, recv_sems):
        self.send_sems, self.recv_sems = send_sems, recv_sems
        self.used = 0
        self.started = []

    def finish(self):
        for phase in self.started:
            phase.whole().wait_send()
        self.started = []


def greet_start(place):
    barrier = pltpu.get_barrier_semaphore()
    for peer in place.peers():
        pl.semaphore_signal(barrier, inc=1, device_id=peer, device_id_type=MESH)


def greet_wait(place):
    pl.semaphore_wait(pltpu.get_barrier_semaphore(), len(place.peers()))


class Spread:
    def __init__(self, place, links, src, dst, rows):
        self.place, self.src, self.dst, self.rows = place, src, dst, rows
        self.phase = Phase(links, dst)

    def start(self):
        p = self.place
        span = pl.ds(pl.multiple_of(p.mp * self.rows, 16), self.rows)
        for t in range(4):
            self.phase.send(table_rows(self.src, t), self.dst.at[span], p.owner(t))

    def wait(self):
        self.phase.wait()


class Collect:
    def __init__(self, place, links, src, dst):
        self.place, self.src, self.dst = place, src, dst
        self.phase = Phase(links, dst)

    def start(self):
        p = self.place
        for s in range(4):
            self.phase.send(table_rows(self.src, s), self.dst.at[p.mp], p.owner(s))

    def wait(self):
        self.phase.wait()


class Gather:
    def __init__(self, place, links, w, unit, per):
        self.place, self.w, self.unit, self.per = place, w, unit, per
        some = w.at[0]
        self.z = Phase(links, some.at[pl.ds(0, 2 * per), pl.ds(0, 32)])
        self.first = Phase(links, some.at[pl.ds(0, 2 * per), pl.ds(0, 96)])
        self.second = Phase(links, some.at[pl.ds(0, 2 * per), pl.ds(0, 384)])
        self.near, self.far = (Phase(links, some.at[pl.ds(0, 2 * per)]) for _ in range(2))

    def piece(self, shard, half, rows, count):
        units = pl.ds(self.unit + self.per * half, self.per)
        return self.w.at[shard, units, pl.ds(pl.multiple_of(rows, 32), count), :]

    def other(self):
        return (1 - self.place.hi) * 2 + self.place.core

    def row(self, half):
        p = self.place
        return p.at(1 - half) * 128 + p.at(half) * 32

    def start(self):
        p = self.place
        for half in range(2):
            view = self.piece(p.mp, half, self.row(half), 32)
            self.z.send(view, view, p.across())

    def start_near(self):
        p = self.place
        whole = self.w.at[p.mp, pl.ds(self.unit, 2 * self.per)]
        self.near.send(whole, whole, p.sibling())

    def step_first(self):
        p = self.place
        self.z.wait()
        for half in range(2):
            view = self.piece(self.other(), half, self.row(half), 32)
            for n in (1, 2, 3):
                self.first.send(view, view, p.along(half, n))

    def step_second(self):
        p = self.place
        self.first.wait()
        for half in range(2):
            view = self.piece(self.other(), half, p.at(1 - half) * 128, 128)
            for n in (1, 2, 3):
                self.second.send(view, view, p.along(1 - half, n))

    def step_last(self):
        self.second.wait()
        view = self.w.at[self.other(), pl.ds(self.unit, 2 * self.per)]
        self.far.send(view, view, self.place.sibling())


class Reduce:
    def __init__(self, place, links, r, unit, per, slots, split):
        self.place, self.r, self.unit, self.per = place, r, unit, per
        self.r1, self.b1, self.r2, self.b2, self.r3 = slots
        self.split = split
        one = r.grads.at[0, 0]
        if split:
            self.plane = [Phase(links, one.at[pl.ds(0, 2 * per), pl.ds(0, 384)]) for _ in range(2)]
        else:
            self.plane = [Phase(links, self.r1)]
        self.line, self.z = Phase(links, self.r2), Phase(links, self.r3)
        self.gather = Phase(links, one.at[pl.ds(0, 2 * per), pl.ds(0, 96)])
        self.gather_more = Phase(links, one.at[pl.ds(0, 2 * per), pl.ds(0, 384)])

    def add(self, k, unit, theirs, count):
        p, r = self.place, self.r

        def one(u, carry):
            mine = r.grads[k, p.core, unit + u].astype(F32)
            r.grads[k, p.core, unit + u] = (mine + theirs[u].astype(F32)).astype(BF)
            return carry

        lax.fori_loop(0, count, one, 0)

    def step_plane(self, k=None):
        p, r = self.place, self.r
        for half in range(2):
            units = pl.ds(self.unit + self.per * half, self.per)
            for n in (1, 2, 3):
                rows = pl.ds(pl.multiple_of(p.at(half, n) * 128, 128), 128)
                if self.split:
                    src, dst = r.grads.at[k, p.core, units, rows, :], self.r1.at[half, n - 1, k]
                else:
                    src, dst = r.grads.at[:, p.core, units, rows, :], self.r1.at[half, n - 1]
                self.plane[k if self.split else 0].send(src, dst, p.along(half, n))

    def step_line(self):
        p, r = self.place, self.r
        for phase in self.plane:
            phase.wait()
        for half in range(2):
            rows = pl.ds(pl.multiple_of(p.at(half) * 128, 128), 128)

            def one(i, carry):
                k, u = lax.div(i, self.per), lax.rem(i, self.per)
                total = r.grads[k, p.core, self.unit + self.per * half + u, rows, :].astype(F32)
                for n in range(3):
                    total = total + self.r1[half, n, k, u].astype(F32)
                self.b1[half, k, u] = total.astype(BF)
                return carry

            lax.fori_loop(0, 2 * self.per, one, 0)
            for n in (1, 2, 3):
                rows = pl.ds(pl.multiple_of(p.at(1 - half, n) * 32, 32), 32)
                src = self.b1.at[half, :, :, rows, :]
                self.line.send(src, self.r2.at[half, n - 1], p.along(1 - half, n))

    def step_z(self):
        p = self.place
        self.line.wait()
        for half in range(2):
            rows = pl.ds(pl.multiple_of(p.at(1 - half) * 32, 32), 32)
            for k in range(2):
                total = self.b1[half, k, :, rows, :].astype(F32)
                for n in range(3):
                    total = total + self.r2[half, n, k].astype(F32)
                self.b2[k, half] = total.astype(BF)
        to = (
            (p.device(lo=1 - p.lo), p.hi),
            (p.device(lo=1 - p.lo, hi=1 - p.hi), 1 - p.hi),
            (p.device(hi=1 - p.hi), 1 - p.hi),
        )
        for n, (device, hi) in enumerate(to):
            self.z.send(self.b2.at[hi], self.r3.at[n], device)

    def kept(self, half, rows, count):
        units = pl.ds(self.unit + self.per * half, self.per)
        return self.r.fin.at[units, pl.ds(pl.multiple_of(rows, 32), count), :]

    def step_spread(self):
        p = self.place
        self.z.wait()
        for half in range(2):
            near = self.b2[p.hi, half].astype(F32) + self.r3[0, half].astype(F32)
            far = self.r3[1, half].astype(F32) + self.r3[2, half].astype(F32)
            view = self.kept(half, p.at(half) * 128 + p.at(1 - half) * 32, 32)
            view[...] = (near + far).astype(BF)
            for n in (1, 2, 3):
                self.gather.send(view, view, p.along(1 - half, n))

    def step_spread_more(self):
        p = self.place
        self.gather.wait()
        for half in range(2):
            view = self.kept(half, p.at(half) * 128, 128)
            for n in (1, 2, 3):
                self.gather_more.send(view, view, p.along(half, n))

    def wait(self):
        self.gather_more.wait()


class Halves:
    def __init__(self, place, links, r, unit, landing):
        self.place, self.r, self.unit, self.landing = place, r, unit, landing
        self.count = landing[0].shape[0]
        self.phases = [Phase(links, view) for view in landing]

    def start(self, k):
        p = self.place
        src = self.r.grads.at[k, 1 - p.core, pl.ds(self.unit, self.count)]
        self.phases[k].send(src, self.landing[k], p.sibling())

    def add(self, reduce, k):
        self.phases[k].wait()
        reduce.add(k, self.unit, self.landing[k], self.count)


class SmallReduce:
    def __init__(self, place, links, r):
        self.place, self.r = place, r
        self.pair = Phase(links, r.sm0)
        self.phases = [Phase(links, slots.at[pl.ds(0, 3)]) for slots in (r.smx, r.smy, r.smz)]

    def start(self):
        p, r = self.place, self.r
        for s in range(4):
            r.sm[s % 2, s // 2, pl.ds(0, 9), :] = r.sums[pl.ds(0, 9), pl.ds(s * 128, 128)]
            r.sm[s % 2, s // 2, pl.ds(9, 6), :] = r.bsums[s, pl.ds(0, 6), :]
            r.sm[s % 2, s // 2, pl.ds(15, 1), :] = jnp.zeros((1, 128), F32)
        self.pair.send(r.sm.at[1 - p.core], r.sm0, p.sibling())

    def step_x(self):
        p, r = self.place, self.r
        self.pair.wait()
        r.smx[p.x] = r.sm[p.core] + r.sm0[...]
        for n in (1, 2, 3):
            self.phases[0].send(r.smx.at[p.x], r.smx.at[p.x], p.along(0, n))

    def step_y(self):
        p, r = self.place, self.r
        self.phases[0].wait()
        r.smy[p.y] = (r.smx[0] + r.smx[1]) + (r.smx[2] + r.smx[3])
        for n in (1, 2, 3):
            self.phases[1].send(r.smy.at[p.y], r.smy.at[p.y], p.along(1, n))

    def step_z(self):
        p, r = self.place, self.r
        self.phases[1].wait()
        mine = p.hi * 2 + p.lo
        r.smz[mine] = (r.smy[0] + r.smy[1]) + (r.smy[2] + r.smy[3])
        for lo, hi in ((1 - p.lo, p.hi), (1 - p.lo, 1 - p.hi), (p.lo, 1 - p.hi)):
            self.phases[2].send(r.smz.at[mine], r.smz.at[mine], p.device(lo=lo, hi=hi))

    def wait(self):
        p, z = self.place, self.r.smz
        self.phases[2].wait()
        total = (z[0, p.hi] + z[1, p.hi]) + (z[2, p.hi] + z[3, p.hi])
        first = 0
        for name in SMALL_OUTS:
            ref = getattr(self.r, name)
            count = ref.shape[0]
            ref[...] = total[first : first + count, :]
            first += count


SMALL_OUTS = ("gout_bias", "gnorm_gain", "gnorm_bias", "gself_qv", "gcross_qv", "gffn_bias")


class Results:
    def __init__(self, r):
        self.r, self.copies = r, []

    def put(self, src, dst):
        copy = pltpu.make_async_copy(src, dst, self.r.out_sems.at[len(self.copies)])
        copy.start()
        self.copies.append(copy)

    def rows(self, tables, pairs, dst, count=None):
        pairs[...] = jnp.swapaxes(tables[...], 0, 1)
        self.put(pairs if count is None else pairs.at[pl.ds(0, count)], dst)

    def units(self, first, count):
        span = pl.ds(first, count)
        self.put(self.r.fin.at[span], self.r.fin_out.at[span])

    def finish(self):
        for copy in self.copies:
            copy.wait()


def load_weights(r, place, sem):
    mp = place.mp
    copies = []

    def put(src, unit, rows=None, count=1):
        if rows is None:
            dst = r.w.at[mp, pl.ds(unit, count)] if count > 1 else r.w.at[mp, unit]
        else:
            dst = r.w.at[mp, unit, pl.ds(rows, 128), :]
        copy = pltpu.make_async_copy(src, dst, sem.at[len(copies)])
        copy.start()
        copies.append(copy)

    put(r.self_qkv, 0, count=3)
    for j in range(4):
        put(r.self_out.at[:, pl.ds(j * 128, 128)], 3, j * 128)
    self_count = len(copies)
    put(r.cross_q, 4)
    copy = pltpu.make_async_copy(r.cross_kv, r.kv_pairs, sem.at[len(copies)])
    copy.start()
    copies.append(copy)
    for j in range(4):
        put(r.cross_out.at[:, pl.ds(j * 128, 128)], 7, j * 128)
    cross_count = len(copies)
    for i in range(2):
        put(r.ffn_in.at[:, pl.ds(i * 128, 128)], 8 + i)
    for i in range(2):
        for j in range(4):
            put(r.ffn_out.at[pl.ds(i * 128, 128), pl.ds(j * 128, 128)], 10 + i, j * 128)
    return copies[:self_count], copies[self_count:cross_count], copies[cross_count:]


LOADS = 24


def by_table(dst, src):
    rows = jnp.swapaxes(src[...], 0, 1)
    if len(dst.shape) == 3:
        dst[...] = rows
    else:
        for t in range(4):
            dst[pl.ds(t * MPAD, MPAD), :] = rows[t]


def table_rows(ref, t):
    return ref.at[t] if len(ref.shape) == 3 else ref.at[pl.ds(t * MPAD, MPAD)]


def layer_kernel(r):
    place = Place()
    links = Links(r.send_sems, r.recv_sems)
    greet_start(place)
    first_loads = []
    for n, (src, dst) in enumerate(
        ((r.tags, r.tags_p), (r.memory, r.mem_p.at[pl.ds(0, MLOC)]), (r.cotangent, r.cot_p))
    ):
        copy = pltpu.make_async_copy(src, dst, r.load_sems.at[LOADS - 3 + n])
        copy.start()
        first_loads.append(copy)
    loads = load_weights(r, place, r.load_sems)

    tags = Spread(place, links, r.tags_t, r.x, L // 4)
    memory = Spread(place, links, r.mem_t, r.m, MPAD)
    cotangent = Spread(place, links, r.cot_t, r.cot, L // 4)
    w_self = Gather(place, links, r.w, 0, 2)
    w_cross, w_ffn = (Gather(place, links, r.w, unit, 2) for unit in (4, 8))
    result = Collect(place, links, r.result, r.result_t)
    tags_grad = Collect(place, links, r.tgrad, r.tgrad_t)
    memory_grad = Collect(place, links, r.mgrad, r.mgrad_t)
    lens = Phase(links, r.lens)
    small_near, small_far = Phase(links, r.small.at[0]), Phase(links, r.small.at[pl.ds(0, 2)])
    def group(unit, per, landing, bufs, n, split=False):
        views = [getattr(r, name).at[n] for name in bufs]
        return Halves(place, links, r, unit, landing), Reduce(place, links, r, unit, per, views, split)

    def freed(first, unit):
        return [r.w.at[first + k, pl.ds(unit, 2)] for k in range(2)]

    one, two = ("s1", "t1", "s2", "t2", "s3"), ("r1", "b1", "r2", "b2", "r3")
    h_out, g_out = group(10, 1, [r.s0.at[k] for k in range(2)], one, 0)
    h_mid, g_mid = group(6, 2, [r.r0.at[k] for k in range(2)], two, 0)
    h_cross, g_cross = group(4, 1, freed(0, 8), one, 1)
    h_value, g_value = group(2, 1, freed(2, 8), one, 2)
    h_query, g_query = group(0, 1, freed(2, 10), one, 3, split=True)
    g_small = SmallReduce(place, links, r)
    assert links.used <= SLOTS
    out = Results(r)

    for t in range(4):
        r.lens_own[pl.ds(t, 1), :] = jnp.full((1, 128), r.tag_lengths[t], jnp.int32)
        r.lens_own[pl.ds(4 + t, 1), :] = jnp.full((1, 128), r.mem_lengths[t], jnp.int32)
    r.small[place.mp, pl.ds(0, 2), :] = r.self_qv_bias[...].astype(F32)
    r.small[place.mp, pl.ds(2, 2), :] = r.cross_qv_bias[...].astype(F32)
    r.small[place.mp, pl.ds(4, 2), :] = r.ffn_in_bias[...].astype(F32)
    r.small[place.mp, pl.ds(6, 2), :] = jnp.zeros((2, 128), F32)
    for n, part in enumerate((r.out_bias, r.norm_gain, r.norm_bias)):
        r.pvec[pl.ds(3 * n, 3), :] = part[...].astype(F32)
    first_loads[0].wait()
    by_table(r.tags_t, r.tags_p)
    greet_wait(place)
    for copy in loads[0]:
        copy.wait()
    w_self.start()
    tags.start()
    lens.send(r.lens_own, r.lens, place.device(lo=1 - place.lo))
    w_self.start_near()
    own = r.small.at[place.mp]
    small_near.send(own, own, place.sibling())
    for core in (place.core, 1 - place.core):
        small_far.send(own, own, place.device(lo=1 - place.lo, hi=1 - place.hi, core=core))
    for copy in loads[1] + loads[2]:
        copy.wait()
    r.w[place.mp, pl.ds(5, 2)] = jnp.swapaxes(r.kv_pairs[...], 0, 1)
    w_cross.start()
    w_ffn.start()
    w_self.step_first()
    first_loads[1].wait()
    r.mem_p[pl.ds(MLOC, MPAD - MLOC)] = jnp.zeros((MPAD - MLOC, 4, D), BF)
    by_table(r.mem_t, r.mem_p)
    memory.start()
    w_cross.start_near()
    w_ffn.start_near()
    w_self.step_second()
    first_loads[2].wait()
    by_table(r.cot_t, r.cot_p)
    cotangent.start()
    w_cross.step_first()
    lens.wait()
    stage_self_mask(r)

    small_near.wait()
    w_self.near.wait()
    tags.wait()
    stage_qkv(r, place.hi)
    w_self.step_last()
    w_cross.step_second()
    w_ffn.step_first()
    stage_self(r, place.hi)
    small_far.wait()
    w_self.far.wait()
    stage_qkv(r, 1 - place.hi)
    w_cross.step_last()
    w_ffn.step_second()
    stage_self(r, 1 - place.hi)
    stage_first(r)
    w_cross.near.wait()
    w_cross.far.wait()
    stage_cross_mask(r)
    stage_cross_q(r)
    memory.wait()
    stage_cross_kv(r)
    w_ffn.step_last()
    stage_cross(r)
    w_ffn.near.wait()
    w_ffn.far.wait()
    kept = stage_rows(r, cotangent.wait)
    links.finish()
    result.start()
    stage_ffn_out_grads(r)
    h_out.start(0)
    h_out.start(1)
    stage_rows_back(r, kept)
    h_out.add(g_out, 0)
    h_out.add(g_out, 1)
    g_out.step_plane()
    stage_ffn_grads(r)
    stage_cross_out_grad(r)
    stage_cross_values(r)
    stage_cross_value_grads(r)
    h_mid.start(0)
    h_mid.start(1)
    g_out.step_line()
    stage_cross_back(r, 0)
    h_mid.add(g_mid, 0)
    h_mid.add(g_mid, 1)
    g_mid.step_plane()
    g_out.step_z()
    stage_cross_back(r, 1)
    g_out.step_spread()
    stage_memory_grad(r)
    memory_grad.start()
    stage_cross_grads(r)
    h_cross.start(0)
    h_cross.start(1)
    g_out.step_spread_more()
    stage_first_back(r)
    h_cross.add(g_cross, 0)
    h_cross.add(g_cross, 1)
    g_cross.step_plane()
    stage_self_out_grad(r)
    stage_self_values(r)
    h_value.start(0)
    h_value.start(1)
    g_mid.step_line()
    stage_self_back(r, 0)
    h_value.add(g_value, 0)
    h_value.add(g_value, 1)
    g_value.step_plane()
    stage_self_grads(r, 0)
    h_query.start(0)
    stage_self_back(r, 1)
    h_query.add(g_query, 0)
    g_query.step_plane(0)
    g_mid.step_z()
    g_cross.step_line()
    stage_self_grads(r, 1)
    h_query.start(1)
    g_small.start()
    stage_tags_grad(r)
    tags_grad.start()
    h_query.add(g_query, 1)
    g_query.step_plane(1)
    g_small.step_x()
    g_mid.step_spread()
    g_cross.step_z()
    g_value.step_line()
    g_out.wait()
    out.units(10, 2)
    result.wait()
    out.rows(r.result_t, r.tags_p, r.result_out)
    g_small.step_y()
    g_query.step_line()
    g_cross.step_spread()
    g_value.step_z()
    g_mid.step_spread_more()
    g_small.step_z()
    memory_grad.wait()
    out.rows(r.mgrad_t, r.mem_p, r.mgrad_out, MLOC)
    g_query.step_z()
    g_value.step_spread()
    g_cross.step_spread_more()
    g_small.wait()
    g_query.step_spread()
    g_value.step_spread_more()
    g_mid.wait()
    out.units(6, 4)
    g_query.step_spread_more()
    g_cross.wait()
    out.units(4, 2)
    tags_grad.wait()
    out.rows(r.tgrad_t, r.cot_p, r.tgrad_out)
    g_value.wait()
    out.units(2, 2)
    g_query.wait()
    out.units(0, 2)
    out.finish()
    links.finish()


def deliver(arrays, outs):
    plain = [name for name in outs if name in arrays]
    made = [name for name in outs if name not in arrays]
    names = plain + ["fin_out"]

    def kernel(*refs):
        refs = list(refs)
        sems = refs.pop()
        srcs = dict(zip(names, refs))
        dsts = dict(zip(outs, refs[len(names) :]))
        held = dict(zip(names + made, refs[len(names) + len(outs) :]))
        reads = {}
        for n, name in enumerate(plain):
            reads[name] = pltpu.make_async_copy(srcs[name], held[name], sems.at[0, n])
            reads[name].start()
        fin = held["fin_out"]
        for n in range(3):
            span = pl.ds(4 * n, 4)
            reads[n] = pltpu.make_async_copy(srcs["fin_out"].at[span], fin.at[span], sems.at[0, len(plain) + n])
            reads[n].start()
        writes = []

        def write(name):
            copy = pltpu.make_async_copy(held[name], dsts[name], sems.at[1, len(writes)])
            copy.start()
            writes.append(copy)

        def blocks(name, first, unit):
            for j in range(4):
                part = fin[unit, pl.ds(j * 128, 128), :].astype(F32)
                held[name][pl.ds(first, 128), pl.ds(j * 128, 128)] = part

        for name in plain:
            reads[name].wait()
            write(name)
        reads[0].wait()
        for j in range(3):
            held["gself_qkv_out"][j] = fin[j].astype(F32)
        write("gself_qkv_out")
        blocks("gself_out_out", 0, 3)
        write("gself_out_out")
        reads[1].wait()
        held["gcross_q_out"][...] = fin[4].astype(F32)
        write("gcross_q_out")
        held["gcross_kv_out"][...] = jnp.swapaxes(fin[pl.ds(5, 2)].astype(F32), 0, 1)
        write("gcross_kv_out")
        blocks("gcross_out_out", 0, 7)
        write("gcross_out_out")
        reads[2].wait()
        for i in range(2):
            held["gffn_in_out"][:, pl.ds(i * 128, 128)] = fin[8 + i].astype(F32)
        write("gffn_in_out")
        for i in range(2):
            blocks("gffn_out_out", i * 128, 10 + i)
        write("gffn_out_out")
        for copy in writes:
            copy.wait()

    hbm = pl.BlockSpec(memory_space=pltpu.HBM)
    shapes = [arrays[name] for name in names] + [outs[name] for name in made]
    return pl.pallas_call(
        kernel,
        out_shape=tuple(outs.values()),
        in_specs=[hbm] * len(names),
        out_specs=(hbm,) * len(outs),
        scratch_shapes=[pltpu.VMEM(a.shape, a.dtype) for a in shapes] + [pltpu.SemaphoreType.DMA((2, len(outs)))],
        compiler_params=pltpu.CompilerParams(vmem_limit_bytes=62 * 1024 * 1024),
        name="deliver",
    )(*[arrays[name] for name in names])


SLOTS = 80


def per_device(
    tags,
    memory,
    cotangent,
    tag_lengths,
    mem_lengths,
    self_qkv,
    self_qv_bias,
    self_out,
    cross_q,
    cross_kv,
    cross_qv_bias,
    cross_out,
    ffn_in,
    ffn_in_bias,
    ffn_out,
    out_bias,
    norm_gain,
    norm_bias,
):
    ins = dict(
        tags=tags,
        memory=memory,
        cotangent=cotangent,
        tag_lengths=tag_lengths,
        mem_lengths=mem_lengths,
        self_qkv=jnp.transpose(self_qkv, (1, 0, 2)),
        self_qv_bias=self_qv_bias,
        self_out=self_out,
        cross_q=cross_q,
        cross_kv=cross_kv,
        cross_qv_bias=cross_qv_bias,
        cross_out=cross_out,
        ffn_in=ffn_in,
        ffn_in_bias=ffn_in_bias.reshape(2, 128),
        ffn_out=ffn_out,
        out_bias=out_bias,
        norm_gain=norm_gain,
        norm_bias=norm_bias,
    )
    in_smem = ("tag_lengths", "mem_lengths")
    in_vmem = ("self_qv_bias", "cross_qv_bias", "ffn_in_bias", "out_bias", "norm_gain", "norm_bias")

    def shape(*dims, dtype=F32):
        return jax.ShapeDtypeStruct(dims, dtype)

    outs = dict(
        result_out=shape(L // 4, 4, D, dtype=BF),
        tgrad_out=shape(L // 4, 4, D, dtype=BF),
        mgrad_out=shape(MLOC, 4, D, dtype=BF),
        gself_qkv_out=shape(3, D, 128),
        gself_qv=shape(2, 128),
        gself_out_out=shape(128, D),
        gcross_q_out=shape(D, 128),
        gcross_kv_out=shape(D, 2, 128),
        gcross_qv=shape(2, 128),
        gcross_out_out=shape(128, D),
        gffn_in_out=shape(D, 256),
        gffn_bias=shape(2, 128),
        gffn_out_out=shape(256, D),
        gout_bias=shape(3, 128),
        gnorm_gain=shape(3, 128),
        gnorm_bias=shape(3, 128),
    )
    own_outs = {name: outs[name] for name in ("result_out", "tgrad_out", "mgrad_out") + SMALL_OUTS}
    own_outs["fin_out"] = shape(12, D, 128, dtype=BF)
    vm = pltpu.VMEM
    scratch = scratch_list()
    scratch.update(
        x=vm((L, D), BF), m=vm((MT, D), BF), cot=vm((L, D), BF),
        lens=vm((8, 128), jnp.int32), lens_own=vm((8, 128), jnp.int32),
        w=vm((4, 12, D, 128), BF), small=vm((4, 8, 128), F32), pvec=vm((16, D), F32),
        tags_p=vm((L // 4, 4, D), BF), mem_p=vm((MPAD, 4, D), BF), cot_p=vm((L // 4, 4, D), BF),
        result=vm((4, L // 4, D), BF), tags_t=vm((4, L // 4, D), BF), mem_t=vm((MT, D), BF), cot_t=vm((4, L // 4, D), BF),
        result_t=vm((4, L // 4, D), BF), mgrad_t=vm((4, MPAD, D), BF), tgrad_t=vm((4, L // 4, D), BF),
        kv_pairs=vm((D, 2, 128), BF), fin=vm((12, D, 128), BF),
        grads=vm((2, 2, 12, D, 128), BF), sums=vm((16, D), F32), bsums=vm((4, 8, 128), F32),
        r0=vm((2, 4, D, 128), BF),
        r1=vm((1, 2, 3, 2, 2, 128, 128), BF), b1=vm((1, 2, 2, 2, 128, 128), BF),
        r2=vm((1, 2, 3, 2, 2, 32, 128), BF), b2=vm((1, 2, 2, 2, 32, 128), BF), r3=vm((1, 3, 2, 2, 32, 128), BF),
        s0=vm((2, 2, D, 128), BF), s1=vm((4, 2, 3, 2, 1, 128, 128), BF), t1=vm((4, 2, 2, 1, 128, 128), BF),
        s2=vm((4, 2, 3, 2, 1, 32, 128), BF), t2=vm((4, 2, 2, 1, 32, 128), BF), s3=vm((4, 3, 2, 1, 32, 128), BF),
        sm=vm((2, 2, 16, 128), F32), sm0=vm((2, 16, 128), F32),
        smx=vm((4, 2, 16, 128), F32), smy=vm((4, 2, 16, 128), F32), smz=vm((4, 2, 16, 128), F32),
        send_sems=pltpu.SemaphoreType.DMA((SLOTS,)),
        recv_sems=pltpu.SemaphoreType.DMA((SLOTS,)),
        load_sems=pltpu.SemaphoreType.DMA((LOADS,)),
        out_sems=pltpu.SemaphoreType.DMA((16,)),
    )
    names = tuple(ins) + tuple(own_outs) + tuple(scratch)
    anywhere = pl.BlockSpec(memory_space=pl.ANY)
    on_chip = pl.BlockSpec(memory_space=pltpu.VMEM)

    def kernel(*refs):
        layer_kernel(Refs(**dict(zip(names, refs))))

    def space(name):
        if name in in_smem:
            return pl.BlockSpec(memory_space=pltpu.SMEM)
        return on_chip if name in in_vmem + SMALL_OUTS else anywhere

    results = pl.pallas_call(
        kernel,
        out_shape=tuple(own_outs.values()),
        in_specs=[space(name) for name in ins],
        out_specs=tuple(space(name) for name in own_outs),
        scratch_shapes=list(scratch.values()),
        compiler_params=pltpu.CompilerParams(
            vmem_limit_bytes=62 * 1024 * 1024, collective_id=0, has_side_effects=True
        ),
        name="layer",
    )(*ins.values())
    results = deliver(dict(zip(own_outs, results)), outs)
    results = dict(zip(outs, results))
    results["gself_qkv_out"] = jnp.transpose(results["gself_qkv_out"], (1, 0, 2))
    results["gffn_bias"] = results["gffn_bias"].reshape(256)
    return tuple(results.values())


def solution(mesh):
    return jax.shard_map(
        per_device,
        mesh=mesh,
        in_specs=(
            P("mp", "dp", None),
            P("mp", "dp", None),
            P("mp", "dp", None),
            P("dp"),
            P("dp"),
            P(None, None, "mp"),
            P(None, "mp"),
            P("mp", None),
            P(None, "mp"),
            P(None, None, "mp"),
            P(None, "mp"),
            P("mp", None),
            P(None, "mp"),
            P("mp"),
            P("mp", None),
            P(),
            P(),
            P(),
        ),
        out_specs=(
            P("mp", "dp", None),
            P("mp", "dp", None),
            P("mp", "dp", None),
            P(None, None, "mp"),
            P(None, "mp"),
            P("mp", None),
            P(None, "mp"),
            P(None, None, "mp"),
            P(None, "mp"),
            P("mp", None),
            P(None, "mp"),
            P("mp"),
            P("mp", None),
            P(None, "mp"),
            P(None, "mp"),
            P(None, "mp"),
        ),
        check_vma=False,
    )
```

time: 984 us -> 98.7 us (0.10)
  waiting for transfers between devices: 691 us -> 0 us
  Pallas kernels: 0 us -> 97.7 us
  blocking collectives: 82.9 us -> 0 us
  matrix products: 77.2 us -> 0 us
  local copies, waits for them, and re-layouts: 62.3 us -> 0 us
  other arithmetic: 43.4 us -> 0 us
  between operations: 16 us -> 0.84 us
    psum x1 -> x0, waiting for transfers between devices: 229 us -> none  [per_device(): lax.psum(grad_self_qkv.astype(jnp.bfloat16), 'dp').astype(jnp.float32)]
    reduce_scatter x6 -> x0, waiting for transfers between devices: 217 us -> none  [the longest x1 37.8 us: per_device(): lax.psum_scatter(first_part.astype(jnp.bfloat16), 'mp', scatter_dimension...]
    all_gather x7 -> x0, waiting for transfers between devices: 159 us -> none  [the longest x1 30.1 us: per_device(): lax.all_gather(memory, 'mp', axis=0, tiled=True)]
    pallas_call x0 -> x2, Pallas kernels: none -> 97.7 us  [the longest x1 94 us: per_device(): pl.pallas_call(kernel, out_shape=tuple(own_outs.values()), in_specs=[spac...]
    unnamed x18 -> x0, waiting for transfers between devices: 85.3 us -> none
    psum x1 -> x0, blocking collectives: 82.9 us -> none  [per_device(): lax.psum(shared_part.astype(jnp.bfloat16), 'dp').astype(jnp.float32)]
    dot_general x33 -> x0, matrix products: 77.2 us -> none  [the longest x2 7.49 us: attend_back(): jnp.einsum('bhqk,qbhe->kbhe', attn_probs.astype(jnp.bfloat16), out_grad,...]
    unnamed x191 -> x0, local copies, waits for them, and re-layouts: 27.2 us -> none
  transfers between devices with their start and end apart: 16 -> 0, of which waited for: 15 -> 0; matrix products, arithmetic and copies ran while one was open for 7% -> 0% of each run, Pallas kernels for 0% -> 0%
where the time goes in v1:
time: 98.7 us; the launch traced here: 98.6 us
  Pallas kernels  97.7 us (99%)
    pallas_call x1, Pallas kernels, per_device(): pl.pallas_call(kernel, out_shape=tuple(own_outs.values()), in_specs=[spac...  94 us
    pallas_call x1, Pallas kernels, deliver(): pl.pallas_call(kernel, out_shape=tuple(outs.values()), in_specs=[hbm] * l...  3.69 us

profile of v1, /device:TPU:0, one launch (start us, length us, event | category | flops | bytes accessed | tf_op | source)
XLA Modules:
  0.0 98.6 jit_solution(4392335966424329289)
XLA Ops:
  0.7 94.0 %layer.1 = (bf16[128,4,512]{2,1,0:T(4,128)(2,1)}, bf16[128,4,512]{2,1,0:T(4,128)(2,1)}, bf16[196,4,512]{2,1,0:T(4,128)(2,1)}, f32[3,128]{1,0:T(4,128)}, f32[3,12...) custom-call(bf16[128,4,512]{2,1,0:T(4,128)(2,1)} %refs_0_.1, ...), custom_call_target="tpu_custom_call" | custom-call | tf_op jit(solution)/shard_map/layer/pallas_call | solution.py:1258
  94.7 3.7 %deliver.1 = (bf16[128,4,512]{2,1,0:T(4,128)(2,1)}, bf16[128,4,512]{2,1,0:T(4,128)(2,1)}, bf16[196,4,512]{2,1,0:T(4,128)(2,1)}, f32[3,512,128]{2,1,0:T(8,128)}, ...) custom-call(bf16[128,4,512]{2,1,0:T(4,128)(2,1)} %get-tuple-element., ...), custom_call_target="tpu_custom_call" | custom-call | tf_op jit(solution)/shard_map/deliver/pallas_call | solution.py:1143

commit v2 on v1

--- a/solution.py
+++ b/solution.py
@@ -993,58 +993,58 @@
     h_out.start(0)
     h_out.start(1)
     stage_rows_back(r, kept)
+    stage_ffn_grads(r)
     h_out.add(g_out, 0)
     h_out.add(g_out, 1)
     g_out.step_plane()
-    stage_ffn_grads(r)
     stage_cross_out_grad(r)
     stage_cross_values(r)
     stage_cross_value_grads(r)
     h_mid.start(0)
     h_mid.start(1)
+    stage_cross_back(r, 0)
     g_out.step_line()
-    stage_cross_back(r, 0)
     h_mid.add(g_mid, 0)
+    stage_cross_back(r, 1)
     h_mid.add(g_mid, 1)
     g_mid.step_plane()
     g_out.step_z()
-    stage_cross_back(r, 1)
-    g_out.step_spread()
     stage_memory_grad(r)
     memory_grad.start()
     stage_cross_grads(r)
     h_cross.start(0)
     h_cross.start(1)
-    g_out.step_spread_more()
+    g_out.step_spread()
     stage_first_back(r)
-    h_cross.add(g_cross, 0)
-    h_cross.add(g_cross, 1)
-    g_cross.step_plane()
     stage_self_out_grad(r)
     stage_self_values(r)
     h_value.start(0)
     h_value.start(1)
+    h_cross.add(g_cross, 0)
+    h_cross.add(g_cross, 1)
+    g_cross.step_plane()
+    g_out.step_spread_more()
+    stage_self_back(r, 0)
     g_mid.step_line()
-    stage_self_back(r, 0)
+    stage_self_grads(r, 0)
+    h_query.start(0)
     h_value.add(g_value, 0)
     h_value.add(g_value, 1)
     g_value.step_plane()
-    stage_self_grads(r, 0)
-    h_query.start(0)
     stage_self_back(r, 1)
-    h_query.add(g_query, 0)
-    g_query.step_plane(0)
+    g_cross.step_line()
     g_mid.step_z()
-    g_cross.step_line()
     stage_self_grads(r, 1)
     h_query.start(1)
     g_small.start()
+    h_query.add(g_query, 0)
+    g_query.step_plane(0)
     stage_tags_grad(r)
     tags_grad.start()
+    g_mid.step_spread()
     h_query.add(g_query, 1)
     g_query.step_plane(1)
     g_small.step_x()
-    g_mid.step_spread()
     g_cross.step_z()
     g_value.step_line()
     g_out.wait()

time: 98.7 us -> 100 us (1.013)
  Pallas kernels: 97.7 us -> 99.2 us
    pallas_call x1, Pallas kernels: 94 us -> 95.5 us  [per_device(): pl.pallas_call(kernel, out_shape=tuple(own_outs.values()), in_specs=[spac...]
where the time goes in v2:
time: 100 us
  Pallas kernels  99.2 us (99%)
    pallas_call x1, Pallas kernels, per_device(): pl.pallas_call(kernel, out_shape=tuple(own_outs.values()), in_specs=[spac...  95.5 us
    pallas_call x1, Pallas kernels, deliver(): pl.pallas_call(kernel, out_shape=tuple(outs.values()), in_specs=[hbm] * l...  3.69 us

profile of v2, /device:TPU:0, one launch (start us, length us, event | category | flops | bytes accessed | tf_op | source)
XLA Modules:
  0.0 100.0 jit_solution(6643548994222221728)
XLA Ops:
  0.7 95.5 %layer.1 = (bf16[128,4,512]{2,1,0:T(4,128)(2,1)}, bf16[128,4,512]{2,1,0:T(4,128)(2,1)}, bf16[196,4,512]{2,1,0:T(4,128)(2,1)}, f32[3,128]{1,0:T(4,128)}, f32[3,12...) custom-call(bf16[128,4,512]{2,1,0:T(4,128)(2,1)} %refs_0_.1, ...), custom_call_target="tpu_custom_call" | custom-call | tf_op jit(solution)/shard_map/layer/pallas_call | solution.py:1258
  96.1 3.7 %deliver.1 = (bf16[128,4,512]{2,1,0:T(4,128)(2,1)}, bf16[128,4,512]{2,1,0:T(4,128)(2,1)}, bf16[196,4,512]{2,1,0:T(4,128)(2,1)}, f32[3,512,128]{2,1,0:T(8,128)}, ...) custom-call(bf16[128,4,512]{2,1,0:T(4,128)(2,1)} %get-tuple-element., ...), custom_call_target="tpu_custom_call" | custom-call | tf_op jit(solution)/shard_map/deliver/pallas_call | solution.py:1143
